TPU v7x, 512 devices: a whole 4x4x16 slice. The times are simulated.
512 devices in a mesh: tile: 32 (over y, x, core), aux: 16 (over z).
Axes of the slice: x: 4, y: 4, z: 16, core: 2. Of those that a mesh axis runs over, the one named last changes fastest.
Arguments:
- amplitudes: bfloat16 [128, 128, 128], P('tile'), may hold values from -6 to 6
- df_factors: bfloat16 [1536, 3072], P('aux'), may hold values from -0.15625 to 0.15625
- out_tiles: int32 [1024], P(('tile', 'aux')), may hold values from 0 to 23
- pair_col: int32 [1024, 16], P(('tile', 'aux')), may hold values from 0 to 23
- pair_amp: int32 [1024, 16], replicated, may hold values from 0 to 127, as said below
Outputs:
- residual: bfloat16 [1024, 128, 128], P(('tile', 'aux'))
Inputs may be any that keep to these rules, and one draw needn't show every extreme that they name: `pair_amp`: among the 32 entries of the output tiles of one device, no owner occurs more than 2 times, and in every device's entries at least one owner occurs exactly 2 times (several may).
All inputs are finite; a program needn't handle non-finite values.
Results may differ from a plain program's by a relative error of at most 0.0049.
Values may be sent and summed in bfloat16 or wider, within the bound.
A program may use at most 128 MiB of HBM per device.

v0:
```python
import jax
import jax.numpy as jnp
from jax import lax
from jax.sharding import PartitionSpec as P


def body(amplitudes, df_factors, out_tiles, pair_col, pair_amp):
    n_tile = lax.axis_size("tile")
    n_aux = lax.axis_size("aux")
    me_tile = lax.axis_index("tile")
    me_aux = lax.axis_index("aux")
    out_count = out_tiles.shape[0]
    pair_count = pair_col.shape[1]
    tile_size = amplitudes.shape[1]
    pair_width = df_factors.shape[1]
    ptiles = pair_width // tile_size
    per_device = out_count * pair_count
    shard_rows = lax.all_gather(df_factors, "aux", axis=0, tiled=True)
    columns = shard_rows.reshape(shard_rows.shape[0], ptiles, tile_size)
    right_side = jnp.take(columns, out_tiles, axis=1)
    assembled = jnp.einsum(
        "qv,qob->ovb", shard_rows, right_side, preferred_element_type=jnp.float32
    )
    gram_rows = assembled.reshape(out_count, ptiles, tile_size, tile_size)
    panels = jnp.take_along_axis(gram_rows, pair_col[:, :, None, None], axis=1).astype(jnp.bfloat16)
    everyone = pair_amp.reshape(n_tile, n_aux, per_device)
    my_lists = lax.dynamic_index_in_dim(everyone, me_aux, 1, keepdims=False)
    own_list = lax.dynamic_index_in_dim(my_lists, me_tile, 0, keepdims=False)
    all_tiles = lax.all_gather(amplitudes, "tile", axis=0, tiled=True)
    picked = jnp.take(all_tiles, own_list, axis=0)
    stacked = picked.reshape(out_count, pair_count, tile_size, tile_size)
    result = jnp.einsum("okac,okcb->oab", stacked, panels, preferred_element_type=jnp.float32)
    return result.astype(jnp.bfloat16)


def solution(mesh):
    in_specs = (
        P("tile", None, None),
        P("aux", None),
        P(("tile", "aux")),
        P(("tile", "aux"), None),
        P(),
    )
    out_specs = P(("tile", "aux"), None, None)
    return jax.shard_map(body, mesh=mesh, in_specs=in_specs, out_specs=out_specs, check_vma=False)
```

profile of v0, /device:TPU:1, one launch (start us, length us, event | category | flops | bytes accessed | tf_op | source)
XLA Modules:
  0.0 227.0 jit_solution(2826224950712772218)
XLA Ops:
  6.5 0.0 all-gather.3.cloned.1.call-start
  6.5 0.7 all-gather.3.cloned.1.call-update
  7.3 0.0 all-gather.5.cloned.1.call-start
  7.3 0.7 all-gather.5.cloned.1.call-update
  8.0 0.7 bitcast_or_fusion
  8.7 0.1 reshape.94
  8.8 1.0 copy.11
  9.8 0.1 reshape.74
  10.0 0.1 squeeze.8
  10.1 0.7 compare_select_fusion.2
  10.8 0.7 compare_and_fusion
  11.4 0.7 compare_and_fusion.1
  12.1 65.5 %all-gather.3.cloned.1.call-done = bf16[128,128,128]{2,1,0:T(8,128)(2,1)} async-done(((bf16[4,128,128]{2,1,0:T(8,128)(2,1)}), bf16[128,128,128]{2,1,0:T(8,128)(2,1)}) %all-gather.3.cloned.1.call-update) | async-done | bytes 4194320 | tf_op jit(solution)/shard_map/all_gather | solution.py:29
  77.6 3.9 %gather_fusion = bf16[32,128,128]{2,1,0:T(8,128)(2,1)} fusion(bf16[128,128,128]{2,1,0:T(8,128)(2,1)} %all-gather.3.cloned.1.call-done, s32[1024]{0:T(1024)S(1)} %pad_clamp_fusion.1), kind=kCustom, calls=%fused_computation | custom fusion | bytes 2097280 | tf_op jit(solution)/shard_map/jit(_take)/gather | solution.py:30
  81.5 113.8 %all-gather.5.cloned.1.call-done = bf16[1536,3072]{1,0:T(8,128)(2,1)} async-done(((bf16[96,3072]{1,0:T(8,128)(2,1)}), bf16[1536,3072]{1,0:T(8,128)(2,1)}) %all-gather.5.cloned.1.call-update) | async-done | bytes 9437200 | tf_op jit(solution)/shard_map/all_gather | solution.py:18
  195.3 9.9 %copy_bitcast_fusion = bf16[1536,24,128]{2,0,1:T(8,128)(2,1)} fusion(bf16[1536,3072]{1,0:T(8,128)(2,1)} %all-gather.5.cloned.1.call-done), kind=kLoop, calls=%fused_computation.3 | loop fusion | bytes 18874368 | tf_op jit(solution)/shard_map/reshape | solution.py:19
  205.2 4.4 %gather_fusion.1 = bf16[2,1536,128]{2,1,0:T(8,128)(2,1)S(1)} fusion(bf16[1536,24,128]{2,0,1:T(8,128)(2,1)} %copy_bitcast_fusion, s32[1024]{0:T(1024)S(1)} %pad_clamp_fusion), kind=kCustom, calls=%fused_computation.1 | custom fusion | bytes 1572872 | tf_op jit(solution)/shard_map/jit(_take)/gather | solution.py:20
  209.6 6.5 %fusion.2 = bf16[2,3072,128]{1,2,0:T(8,128)(2,1)S(1)} fusion(bf16[1536,3072]{1,0:T(8,128)(2,1)} %all-gather.5.cloned.1.call-done, bf16[2,1536,128]{2,1,0:T(8,128)(2,1)S(1)} %gather_fusion.1, pred[2]{0:T(512)(128)(4,1)S(1)} %compare_and_fusion), kind=kOutput, calls=%fused_computation.6 | convolution fusion | flops 2416312320 | bytes 11796482 | tf_op jit(solution)/shard_map/qv,qob->ovb/dot_general | solution.py:21
  216.1 0.9 copy.17
  217.0 0.8 gather_fusion.2
  217.8 2.4 %fusion.5 = bf16[2,128,128]{2,1,0:T(8,128)(2,1)} fusion(bf16[2,16,128,128]{3,2,1,0:T(8,128)(2,1)S(1)} %bitcast.33, bf16[2,16,128,128]{3,2,1,0:T(8,128)(2,1)} %bitcast.32, pred[2,16]{1,0:T(4,128)(4,1)S(1)} %get-tuple-element.5, pred[2,16]{1,0:T(4,128)(4,1)S(1)} %get-tuple-element.6), kind=kOutput, calls=%fused_computation.9 | convolution fusion | flops 135299072 | bytes 2162752 | tf_op jit(solution)/shard_map/okac,okcb->oab/dot_general | solution.py:32
  (4 shorter events, 0.0 us)
Async XLA Ops:
  6.5 71.1 %all-gather.3.cloned.1.call-start = ((), (), s32[]{:S(2)}) async-start(), calls=%async_computation | async-start | bytes 4325376 | tf_op jit(solution)/shard_map/all_gather | solution.py:29
  7.3 188.0 %all-gather.5.cloned.1.call-start = ((), (), s32[]{:S(2)}) async-start(), calls=%async_computation.1 | async-start | bytes 10027008 | tf_op jit(solution)/shard_map/all_gather | solution.py:18
Sparse Core Ops, SparseCore 0:
  10.5 67.0 all-gather.2
  79.7 115.5 all-gather.4
where the time goes:
time: 227 us
  waiting for transfers between devices  181 us (80%)
  local copies, waits for them, and re-layouts  21.2 us (9%)
  between operations  13.5 us (6%)
  matrix products  8.9 us (4%)
  other arithmetic  2.72 us (1%)
    all_gather x1, waiting for transfers between devices, body(): shard_rows = lax.all_gather(df_factors, 'aux', axis=0, tiled=True)  114 us
    all_gather x1, waiting for transfers between devices, body(): all_tiles = lax.all_gather(amplitudes, 'tile', axis=0, tiled=True)  65.5 us
    reshape x1, local copies, waits for them, and re-layouts, body(): columns = shard_rows.reshape(shard_rows.shape[0], ptiles, tile_size)  9.91 us
    dot_general x1, matrix products, body(): jnp.einsum('qv,qob->ovb', shard_rows, right_side, preferred_element_type=...  6.51 us
  transfers between devices with their start and end apart: 2, of which 2 were waited for; matrix products, arithmetic and copies ran while one was open for 3% of the time, Pallas kernels for 0%

commit v1 on v0

v1 whole, which is shorter than its diff:
```python
import functools

import jax
import jax.numpy as jnp
from jax import lax
from jax.experimental import pallas as pl
from jax.experimental.pallas import tpu as pltpu
from jax.sharding import PartitionSpec as P

MESH = pl.DeviceIdType.MESH
NX = 4
NY = 4
LINE = 4
QUAD = 4
NT = (((1,), (1,)), ((), ()))
NN = (((1,), (0,)), ((), ()))


def kernel(amp_ref, list_ref, a_ref, b_ref, out_ref,
           a_all, b_all, lists_v, lists_s, own, part_s, part_r,
           loc_sem, z_send, z_recv, l_send, l_recv,
           a_send, a_fsend, a_csend, a_recv, a_crecv,
           b_send, b_fsend, b_csend, b_recv, b_crecv,
           r_send, r_recv):
    tile = lax.axis_index("tile")
    z = lax.axis_index("aux")
    core = lax.rem(tile, 2)
    x = lax.rem(tile // 2, NX)
    y = tile // (2 * NX)
    pos = lax.rem(z, LINE)
    base = z - pos
    rows = b_ref.shape[0]
    ctiles = b_all.shape[0]
    nb = ctiles // (2 * NX)
    far = b_all.shape[1] - rows
    half = far // 2

    def at(xx, yy, cc):
        return (yy * NX + xx) * 2 + cc

    def xp(i):
        return lax.rem(x + i, NX)

    def yp(i):
        return lax.rem(y + i, NY)

    def xdev(i):
        return (at(xp(i), y, core), z)

    def ydev(i):
        return (at(x, yp(i), core), z)

    def zdev(i):
        return (tile, lax.rem(z + LINE * i, LINE * QUAD))

    def ldev(i):
        return (tile, base + lax.rem(pos + i, LINE))

    sib = (at(x, y, 1 - core), z)

    def remote(src, dst, ss, rs, dev):
        return pltpu.make_async_remote_copy(
            src_ref=src, dst_ref=dst, send_sem=ss, recv_sem=rs, device_id=dev, device_id_type=MESH)

    def apiece(d, h):
        return a_all.at[pl.ds(d * 4 + 2 * h, 2)]

    def bpiece(d, h):
        return b_all.at[d, pl.ds(rows + half * h, half)]

    own_a = pltpu.make_async_copy(a_ref, a_all.at[pl.ds(tile * 4, 4)], loc_sem.at[0])
    own_a.start()
    b_copies = []
    for c in range(ctiles):
        cp = pltpu.make_async_copy(
            b_ref.at[:, pl.ds(c * 128, 128)], b_all.at[c, pl.ds(0, rows)], loc_sem.at[2 + c])
        cp.start()
        b_copies.append(cp)
    lists_v[pos] = list_ref[...]

    barrier = pltpu.get_barrier_semaphore()
    devs = [f(i) for i in (1, 2, 3) for f in (xdev, ydev, zdev, ldev)] + [sib]
    for dev in devs:
        pl.semaphore_signal(barrier, inc=1, device_id=dev, device_id_type=MESH)
    own_a.wait()
    for cp in b_copies:
        cp.wait()
    pl.semaphore_wait(barrier, len(devs))

    def zcopy(i):
        return remote(b_all.at[tile, pl.ds(0, rows)], b_all.at[tile, pl.ds(rows * (QUAD - i), rows)],
                      z_send.at[i], z_recv.at[QUAD - i], zdev(i))

    def zwait(r):
        return remote(b_all.at[tile, pl.ds(0, rows)], b_all.at[tile, pl.ds(rows * r, rows)],
                      z_send.at[r], z_recv.at[r], zdev(r))

    @pl.when(y < nb)
    def _():
        for i in (2, 1, 3):
            zcopy(i).start()

    def lcopy(i):
        return remote(lists_v.at[pos], lists_v.at[pos], l_send.at[i], l_recv.at[i], ldev(i))

    def lwait(i):
        j = lax.rem(pos + i, LINE)
        return remote(lists_v.at[j], lists_v.at[j], l_send.at[i], l_recv.at[LINE - i], ldev(i))

    def asend(h, k, i, dev):
        return remote(apiece(tile, h), apiece(tile, h), a_send.at[h, k, i], a_recv.at[h, tile // 2], dev)

    for i in (1, 3, 2):
        asend(0, 0, i, xdev(i)).start()
        asend(1, 1, i, ydev(i)).start()
    for i in (1, 3, 2):
        asend(0, 1, i, ydev(i)).start()
        asend(1, 0, i, xdev(i)).start()
    for i in (1, 2, 3):
        lcopy(i).start()

    def whole(d):
        return a_all.at[pl.ds(d * 4, 4)]

    def acore(d):
        return remote(whole(d), whole(d), a_csend.at[d // 2], a_crecv.at[d // 2], sib)

    acore(tile).start()

    def await_a(d, h):
        remote(apiece(d, h), apiece(d, h), a_send.at[0, 0, 0], a_recv.at[h, d // 2], sib).wait_recv()

    def afwd(h, j, i, d, dev):
        return remote(apiece(d, h), apiece(d, h), a_fsend.at[h, j, i], a_recv.at[h, d // 2], dev)

    for j in (1, 3, 2):
        d = at(xp(j), y, core)
        await_a(d, 0)
        for i in (1, 3, 2):
            afwd(0, j, i, d, ydev(i)).start()
        d = at(x, yp(j), core)
        await_a(d, 1)
        for i in (1, 3, 2):
            afwd(1, j, i, d, xdev(i)).start()

    def bsend(h, k, i, dev):
        return remote(bpiece(tile, h), bpiece(tile, h), b_send.at[h, k, i], b_recv.at[h, tile // 2], dev)

    def bwhole(d):
        return b_all.at[d, pl.ds(rows, far)]

    def bcore(d):
        return remote(bwhole(d), bwhole(d), b_csend.at[d // 2], b_crecv.at[d // 2], sib)

    def await_b(d, h):
        remote(bpiece(d, h), bpiece(d, h), b_send.at[0, 0, 0], b_recv.at[h, d // 2], sib).wait_recv()

    def bfwd(h, j, i, d, dev):
        return remote(bpiece(d, h), bpiece(d, h), b_fsend.at[h, j, i], b_recv.at[h, d // 2], dev)

    @pl.when(y < nb)
    def _():
        for r in (1, 2, 3):
            zwait(r).wait_recv()
        for i in (1, 3, 2):
            bsend(0, 0, i, xdev(i)).start()
            bsend(1, 1, i, ydev(i)).start()
        for i in (1, 3, 2):
            bsend(0, 1, i, ydev(i)).start()
            bsend(1, 0, i, xdev(i)).start()
        bcore(tile).start()

    for j in (1, 3, 2):
        @pl.when(y < nb)
        def _():
            d = at(xp(j), y, core)
            await_b(d, 0)
            for i in (1, 3, 2):
                bfwd(0, j, i, d, ydev(i)).start()

        @pl.when(yp(j) < nb)
        def _():
            d = at(x, yp(j), core)
            await_b(d, 1)
            for i in (1, 3, 2):
                bfwd(1, j, i, d, xdev(i)).start()

    def rest_a(d, first, second):
        if first:
            await_a(d, 0)
        if second:
            await_a(d, 1)
        acore(d).start()

    for j in (1, 2, 3):
        rest_a(at(xp(j), y, core), False, True)
        rest_a(at(x, yp(j), core), True, False)
    for i in (1, 2, 3):
        for j in (1, 2, 3):
            rest_a(at(xp(j), yp(i), core), True, True)

    def rest_b(yy, d, first, second):
        @pl.when(yy < nb)
        def _():
            if first:
                await_b(d, 0)
            if second:
                await_b(d, 1)
            bcore(d).start()

    for j in (1, 2, 3):
        rest_b(y, at(xp(j), y, core), False, True)
        rest_b(yp(j), at(x, yp(j), core), True, False)
    for i in (1, 2, 3):
        for j in (1, 2, 3):
            rest_b(yp(i), at(xp(j), yp(i), core), True, True)

    for i in (1, 2, 3):
        lwait(i).wait_recv()
    lists = pltpu.make_async_copy(lists_v, lists_s, loc_sem.at[1])
    lists.start()

    def from_core_a(n, _):
        d = n * 2 + 1 - core
        remote(whole(d), whole(d), a_csend.at[n], a_crecv.at[n], sib).wait_recv()
        return 0

    lax.fori_loop(0, NX * NY, from_core_a, 0)

    def from_core_b(n, _):
        d = n * 2 + 1 - core
        remote(bwhole(d), bwhole(d), b_csend.at[n], b_crecv.at[n], sib).wait_recv()
        return 0

    lax.fori_loop(0, nb * NX, from_core_b, 0)
    lists.wait()

    def partial(p, o):
        total = None
        for k in range(0, 16, 2):
            am = jnp.concatenate([a_all[amp_ref[2 * p + o, k + s]] for s in (0, 1)], axis=1)
            bm = jnp.concatenate([b_all[lists_s[p, o, k + s]] for s in (0, 1)], axis=1)
            term = lax.dot_general(am, bm, NT, preferred_element_type=jnp.float32)
            total = term if total is None else total + term
        right = b_all[lists_s[p, 2 + o, 0]]
        return lax.dot_general(total.astype(jnp.bfloat16), right, NN, preferred_element_type=jnp.float32)

    def rcopy(n, i, o):
        return remote(part_s.at[n], part_r.at[n], r_send.at[n], r_recv.at[n], ldev(i))

    def away(n, _):
        i = n // 2 + 1
        o = lax.rem(n, 2)
        part_s[n] = partial(lax.rem(pos + i, LINE), o).astype(jnp.bfloat16)
        rcopy(n, i, o).start()
        return 0

    lax.fori_loop(0, 6, away, 0)

    def home(o, _):
        own[o] = partial(pos, o)
        return 0

    lax.fori_loop(0, 2, home, 0)

    for n in range(6):
        rcopy(n, n // 2 + 1, n % 2).wait_recv()
    for o in range(2):
        out_ref[o] = (own[o] + part_r[o].astype(jnp.float32) + part_r[2 + o].astype(jnp.float32)
                      + part_r[4 + o].astype(jnp.float32)).astype(jnp.bfloat16)

    for n in range(6):
        rcopy(n, n // 2 + 1, n % 2).wait_send()
    for i in (1, 2, 3):
        lcopy(i).wait_send()
        for h in (0, 1):
            asend(h, 0, i, xdev(i)).wait_send()
            asend(h, 1, i, ydev(i)).wait_send()
            for j in (1, 2, 3):
                if h == 0:
                    afwd(0, j, i, at(xp(j), y, core), ydev(i)).wait_send()
                else:
                    afwd(1, j, i, at(x, yp(j), core), xdev(i)).wait_send()

    def core_sent(n, _):
        acore(n * 2 + core).wait_send()
        return 0

    lax.fori_loop(0, NX * NY, core_sent, 0)

    def bcore_sent(n, _):
        bcore(n * 2 + core).wait_send()
        return 0

    lax.fori_loop(0, nb * NX, bcore_sent, 0)

    @pl.when(y < nb)
    def _():
        for i in (1, 2, 3):
            zcopy(i).wait_send()
            for h in (0, 1):
                bsend(h, 0, i, xdev(i)).wait_send()
                bsend(h, 1, i, ydev(i)).wait_send()
            for j in (1, 2, 3):
                bfwd(0, j, i, at(xp(j), y, core), ydev(i)).wait_send()

    for j in (1, 2, 3):
        @pl.when(yp(j) < nb)
        def _():
            for i in (1, 2, 3):
                bfwd(1, j, i, at(x, yp(j), core), xdev(i)).wait_send()


def body(amplitudes, df_factors, out_tiles, pair_col, pair_amp):
    me_tile = lax.axis_index("tile")
    me_aux = lax.axis_index("aux")
    ts = amplitudes.shape[1]
    rows, cols = df_factors.shape
    ctiles = cols // ts
    start = (me_tile * 16 + (me_aux // LINE) * LINE) * 2
    amps = lax.dynamic_slice_in_dim(pair_amp, start, 2 * LINE, 0)
    lists = jnp.concatenate([pair_col, jnp.broadcast_to(out_tiles[:, None], pair_col.shape)], axis=0)
    lists = jnp.pad(lists, ((0, 4), (0, 128 - pair_col.shape[1])))
    dma = pltpu.SemaphoreType.DMA
    chips = NX * NY
    vmem = pl.BlockSpec(memory_space=pltpu.VMEM)
    anyw = pl.BlockSpec(memory_space=pl.ANY)
    return pl.pallas_call(
        kernel,
        out_shape=jax.ShapeDtypeStruct((2, ts, ts), jnp.bfloat16),
        in_specs=[pl.BlockSpec(memory_space=pltpu.SMEM), vmem, anyw, anyw],
        out_specs=vmem,
        scratch_shapes=[
            pltpu.VMEM((128, ts, ts), jnp.bfloat16),
            pltpu.VMEM((ctiles, QUAD * rows, ts), jnp.bfloat16),
            pltpu.VMEM((LINE, 8, 128), jnp.int32),
            pltpu.SMEM((LINE, 8, 128), jnp.int32),
            pltpu.VMEM((2, ts, ts), jnp.float32),
            pltpu.VMEM((6, ts, ts), jnp.bfloat16),
            pltpu.VMEM((6, ts, ts), jnp.bfloat16),
            dma((2 + ctiles,)), dma((4,)), dma((4,)), dma((4,)), dma((4,)),
            dma((2, 2, 4)), dma((2, 4, 4)), dma((chips,)), dma((2, chips)), dma((chips,)),
            dma((2, 2, 4)), dma((2, 4, 4)), dma((chips,)), dma((2, chips)), dma((chips,)),
            dma((6,)), dma((6,)),
        ],
        compiler_params=pltpu.CompilerParams(
            collective_id=0, has_side_effects=True, vmem_limit_bytes=40 * 2**20),
        name="residual",
    )(amps, lists, amplitudes, df_factors)


def solution(mesh):
    in_specs = (
        P("tile", None, None),
        P("aux", None),
        P(("tile", "aux")),
        P(("tile", "aux"), None),
        P(),
    )
    out_specs = P(("tile", "aux"), None, None)
    return jax.shard_map(body, mesh=mesh, in_specs=in_specs, out_specs=out_specs, check_vma=False)
```

time: 227 us -> 59.5 us (0.26)
  waiting for transfers between devices: 181 us -> 0 us
  Pallas kernels: 0 us -> 55.1 us
  local copies, waits for them, and re-layouts: 21.2 us -> 4.12 us
  between operations: 13.5 us -> 0.02 us
  matrix products: 8.9 us -> 0 us
  other arithmetic: 2.72 us -> 0.07 us
    all_gather x2 -> x0, waiting for transfers between devices: 179 us -> none  [the longest x1 114 us: body(): shard_rows = lax.all_gather(df_factors, 'aux', axis=0, tiled=True)]
    pallas_call x0 -> x1, Pallas kernels: none -> 55.1 us  [body(): pl.pallas_call(kernel, out_shape=jax.ShapeDtypeStruct((2, ts, ts), jnp.bf...]
    reshape x3 -> x0, local copies, waits for them, and re-layouts: 11 us -> none  [the longest x1 9.91 us: body(): columns = shard_rows.reshape(shard_rows.shape[0], ptiles, tile_size)]
    gather x4 -> x0, local copies, waits for them, and re-layouts: 9.07 us -> none  [the longest x1 4.38 us: body(): right_side = jnp.take(columns, out_tiles, axis=1)]
    dot_general x2 -> x0, matrix products: 8.9 us -> none  [the longest x1 6.51 us: body(): jnp.einsum('qv,qob->ovb', shard_rows, right_side, preferred_element_type=...]
    unnamed x1 -> x12, local copies, waits for them, and re-layouts: 1.03 us -> 3.97 us
  transfers between devices with their start and end apart: 2 -> 0, of which waited for: 2 -> 0; matrix products, arithmetic and copies ran while one was open for 3% -> 0% of each run, Pallas kernels for 0% -> 0%
where the time goes in v1:
time: 59.5 us; the launch traced here: 59.3 us
  Pallas kernels  55.1 us (93%)
  local copies, waits for them, and re-layouts  4.12 us (7%)
    pallas_call x1, Pallas kernels, body(): pl.pallas_call(kernel, out_shape=jax.ShapeDtypeStruct((2, ts, ts), jnp.bf...  55.1 us
    unnamed x12, local copies, waits for them, and re-layouts  3.97 us

profile of v1, /device:TPU:1, one launch (start us, length us, event | category | flops | bytes accessed | tf_op | source)
XLA Modules:
  0.0 59.3 jit_solution(563713889397348706)
XLA Ops:
  0.0 0.0 copy-start
  0.0 0.0 copy-start.4
  0.0 0.7 %copy-done.4 = s32[2]{0:T(128)S(1)} copy-done((s32[2]{0:T(128)S(1)}, s32[2]{0:T(128)}, u32[]{:S(2)}) %copy-start.4) | copy-done | bytes 32
  0.7 0.0 copy-start.3
  0.7 0.1 pad.6.clone
  0.8 0.6 %copy-done.3 = s32[2,16]{1,0:T(2,128)S(1)} copy-done((s32[2,16]{1,0:T(2,128)S(1)}, s32[2,16]{1,0:T(2,128)}, u32[]{:S(2)}) %copy-start.3) | copy-done | bytes 152
  1.4 0.1 pad_add_fusion
  1.4 0.0 copy-done
  1.5 0.1 constant_dynamic-slice_fusion
  1.5 0.1 copy.7.amp_ref
  1.6 0.0 copy-start.1
  1.6 1.1 %copy-done.1 = bf16[96,3072]{1,0:T(8,128)(2,1)S(1)} copy-done((bf16[96,3072]{1,0:T(8,128)(2,1)S(1)}, bf16[96,3072]{1,0:T(8,128)(2,1)}, u32[]{:S(2)}) %copy-start.1) | copy-done | bytes 589848
  2.7 0.0 copy-start.2
  2.7 0.9 %copy-done.2 = bf16[4,128,128]{2,1,0:T(8,128)(2,1)S(1)} copy-done((bf16[4,128,128]{2,1,0:T(8,128)(2,1)S(1)}, bf16[4,128,128]{2,1,0:T(8,128)(2,1)}, u32[]{:S(2)}) %copy-start.2) | copy-done | bytes 131096
  3.6 55.1 %residual.1 = bf16[2,128,128]{2,1,0:T(8,128)(2,1)S(1)} custom-call(s32[8,16]{1,0:T(8,128)S(1)} %copy.7.amp_ref, s32[8,128]{1,0:T(8,128)S(1)} %pad.4.list_ref, bf16[4,128,128]{2,1,0:T(8,128)(2,1)S(1)} %copy-done.2, bf16[96,3072]{1,0:T(8,128)(2,1)S(1)} %copy-done.1), custom_call_target="tpu_custom_call" | custom-call | tf_op jit(solution)/shard_map/residual/pallas_call | solution.py:328
  58.7 0.6 %copy.9 = bf16[2,128,128]{2,1,0:T(8,128)(2,1)} copy(bf16[2,128,128]{2,1,0:T(8,128)(2,1)S(1)} %residual.1) | data formatting | bytes 131072
  (1 shorter events, 0.0 us)
Async XLA Ops:
  0.0 1.5 %copy-start = (s32[1024,16]{0,1:T(8,128)S(1)}, s32[1024,16]{0,1:T(8,128)}, u32[]{:S(2)}) copy-start(s32[1024,16]{0,1:T(8,128)} %param.9) | copy-start | bytes 196612
  0.0 0.7 %copy-start.4 = (s32[2]{0:T(128)S(1)}, s32[2]{0:T(128)}, u32[]{:S(2)}) copy-start(s32[2]{0:T(128)} %param.7) | copy-start | bytes 28
  0.7 0.7 %copy-start.3 = (s32[2,16]{1,0:T(2,128)S(1)}, s32[2,16]{1,0:T(2,128)}, u32[]{:S(2)}) copy-start(s32[2,16]{1,0:T(2,128)} %param.8) | copy-start | bytes 388
  1.6 1.1 %copy-start.1 = (bf16[96,3072]{1,0:T(8,128)(2,1)S(1)}, bf16[96,3072]{1,0:T(8,128)(2,1)}, u32[]{:S(2)}) copy-start(bf16[96,3072]{1,0:T(8,128)(2,1)} %b_ref.1) | copy-start | bytes 1769476
  2.7 0.9 %copy-start.2 = (bf16[4,128,128]{2,1,0:T(8,128)(2,1)S(1)}, bf16[4,128,128]{2,1,0:T(8,128)(2,1)}, u32[]{:S(2)}) copy-start(bf16[4,128,128]{2,1,0:T(8,128)(2,1)} %a_ref.1) | copy-start | bytes 393220

commit v2 on v1

v2 whole, which is shorter than its diff:
```python
import functools

import jax
import jax.numpy as jnp
from jax import lax
from jax.experimental import pallas as pl
from jax.experimental.pallas import tpu as pltpu
from jax.sharding import PartitionSpec as P

MESH = pl.DeviceIdType.MESH
NX = 4
NY = 4
LINE = 4
QUAD = 4
NT = (((1,), (1,)), ((), ()))
NN = (((1,), (0,)), ((), ()))


def kernel(amp_ref, col_ref, tgt_ref, a_ref, b_ref, out_ref,
           a_all, b_all, cols_v, tgts_v, amp_s, cols_s, tgts_s, own, part_s, part_r,
           loc_sem, z_ack, l_ack, z_send, z_recv, l_send, l_recv,
           a_send, a_fsend, a_csend, a_recv, a_crecv,
           b_send, b_fsend, b_csend, b_recv, b_crecv,
           r_send, r_recv):
    tile = lax.axis_index("tile")
    z = lax.axis_index("aux")
    core = lax.rem(tile, 2)
    x = lax.rem(tile // 2, NX)
    y = tile // (2 * NX)
    pos = lax.rem(z, LINE)
    rank = z // LINE
    base = z - pos
    rows = b_ref.shape[0]
    ctiles = b_all.shape[0]
    nb = ctiles // (2 * NX)
    first = (rows, 2 * rows)
    count = (rows, 2 * rows)

    def at(xx, yy, cc):
        return (yy * NX + xx) * 2 + cc

    def xp(i):
        return lax.rem(x + i, NX)

    def yp(i):
        return lax.rem(y + i, NY)

    def xdev(i):
        return (at(xp(i), y, core), z)

    def ydev(i):
        return (at(x, yp(i), core), z)

    def zdev(i):
        return (tile, lax.rem(z + LINE * i, LINE * QUAD))

    def ldev(i):
        return (tile, base + lax.rem(pos + i, LINE))

    sib = (at(x, y, 1 - core), z)
    mine = (tile * LINE * QUAD + base) * 2

    def remote(src, dst, ss, rs, dev):
        return pltpu.make_async_remote_copy(
            src_ref=src, dst_ref=dst, send_sem=ss, recv_sem=rs, device_id=dev, device_id_type=MESH)

    def signal(sem, dev):
        pl.semaphore_signal(sem, inc=1, device_id=dev, device_id_type=MESH)

    local = [
        pltpu.make_async_copy(a_ref, a_all.at[pl.ds(tile * 4, 4)], loc_sem.at[0]),
        pltpu.make_async_copy(col_ref, cols_v.at[pos], loc_sem.at[1]),
        pltpu.make_async_copy(tgt_ref, tgts_v.at[pos], loc_sem.at[2]),
        pltpu.make_async_copy(
            amp_ref.at[:, pl.ds(pl.multiple_of(mine - lax.rem(mine, 128), 128), 128)], amp_s, loc_sem.at[3]),
    ]
    for c in range(ctiles):
        local.append(pltpu.make_async_copy(
            b_ref.at[:, pl.ds(c * 128, 128)], b_all.at[c, pl.ds(0, rows)], loc_sem.at[6 + c]))

    barrier = pltpu.get_barrier_semaphore()
    near = [f(i) for i in (1, 2, 3) for f in (xdev, ydev)] + [sib]
    for dev in near:
        signal(barrier, dev)
    for i in (1, 2, 3):
        @pl.when(rank + i < QUAD)
        def _():
            signal(barrier, zdev(i))

        @pl.when(pos + i < LINE)
        def _():
            signal(barrier, ldev(i))
    for cp in local:
        cp.start()
    for cp in local:
        cp.wait()
    pl.semaphore_wait(barrier, len(near) + rank + pos)
    for i in (1, 2, 3):
        @pl.when(rank + i >= QUAD)
        def _():
            signal(z_ack.at[QUAD - i], zdev(i))

        @pl.when(pos + i >= LINE)
        def _():
            signal(l_ack.at[LINE - i], ldev(i))

    def zcopy(i):
        return remote(b_all.at[tile, pl.ds(0, rows)], b_all.at[tile, pl.ds(rows * (QUAD - i), rows)],
                      z_send.at[i], z_recv.at[QUAD - i], zdev(i))

    def zwait(r):
        remote(b_all.at[tile, pl.ds(0, rows)], b_all.at[tile, pl.ds(rows * r, rows)],
               z_send.at[r], z_recv.at[r], zdev(r)).wait_recv()

    def zup(i, ranks):
        for r in ranks:
            @pl.when(rank == r)
            def _():
                pl.semaphore_wait(z_ack.at[i], 1)

                @pl.when(y < nb)
                def _():
                    zcopy(i).start()

    for i in (2, 1, 3):
        @pl.when((rank + i >= QUAD) & (y < nb))
        def _():
            zcopy(i).start()

    def lcopies(i):
        return [remote(v.at[pos], v.at[pos], l_send.at[n, i], l_recv.at[n, i], ldev(i))
                for n, v in enumerate((cols_v, tgts_v))]

    def lwaits(i):
        j = lax.rem(pos + i, LINE)
        for n, v in enumerate((cols_v, tgts_v)):
            remote(v.at[j], v.at[j], l_send.at[n, i], l_recv.at[n, LINE - i], ldev(i)).wait_recv()

    def apiece(d, h):
        return a_all.at[pl.ds(d * 4 + 2 * h, 2)]

    def whole(d):
        return a_all.at[pl.ds(d * 4, 4)]

    def asend(h, k, i, dev):
        return remote(apiece(tile, h), apiece(tile, h), a_send.at[h, k, i], a_recv.at[h, tile // 2], dev)

    def acore(d):
        return remote(whole(d), whole(d), a_csend.at[d // 2], a_crecv.at[d // 2], sib)

    def await_a(d, h):
        remote(apiece(d, h), apiece(d, h), a_send.at[0, 0, 0], a_recv.at[h, d // 2], sib).wait_recv()

    def afwd(h, j, i, d, dev):
        return remote(apiece(d, h), apiece(d, h), a_fsend.at[h, j, i], a_recv.at[h, d // 2], dev)

    for i in (1, 3, 2):
        asend(0, 0, i, xdev(i)).start()
        asend(1, 1, i, ydev(i)).start()
    for i in (1, 3, 2):
        asend(0, 1, i, ydev(i)).start()
        asend(1, 0, i, xdev(i)).start()
    for i in (1, 2, 3):
        @pl.when(pos + i >= LINE)
        def _():
            for cp in lcopies(i):
                cp.start()
    acore(tile).start()

    for j in (1, 3, 2):
        d = at(xp(j), y, core)
        await_a(d, 0)
        for i in (1, 3, 2):
            afwd(0, j, i, d, ydev(i)).start()
        d = at(x, yp(j), core)
        await_a(d, 1)
        for i in (1, 3, 2):
            afwd(1, j, i, d, xdev(i)).start()

    zup(1, (0, 1, 2))
    zup(2, (1,))
    for i in (1, 2, 3):
        @pl.when(pos + i < LINE)
        def _():
            pl.semaphore_wait(l_ack.at[i], 1)
            for cp in lcopies(i):
                cp.start()

    def bpiece(s, d, h):
        return b_all.at[d, pl.ds(first[s] + count[s] // 2 * h, count[s] // 2)]

    def bwhole(s, d):
        return b_all.at[d, pl.ds(first[s], count[s])]

    def bsend(s, h, k, i, dev):
        return remote(bpiece(s, tile, h), bpiece(s, tile, h), b_send.at[s, h, k, i], b_recv.at[s, h, tile // 2], dev)

    def bcore(s, d):
        return remote(bwhole(s, d), bwhole(s, d), b_csend.at[s, d // 2], b_crecv.at[s, d // 2], sib)

    def await_b(s, d, h):
        remote(bpiece(s, d, h), bpiece(s, d, h), b_send.at[s, 0, 0, 0], b_recv.at[s, h, d // 2], sib).wait_recv()

    def bfwd(s, h, j, i, d, dev):
        return remote(bpiece(s, d, h), bpiece(s, d, h), b_fsend.at[s, h, j, i], b_recv.at[s, h, d // 2], dev)

    def b_own(s):
        @pl.when(y < nb)
        def _():
            for r in ((1,), (2, 3))[s]:
                zwait(r)
            for i in (1, 3, 2):
                bsend(s, 0, 0, i, xdev(i)).start()
                bsend(s, 1, 1, i, ydev(i)).start()
            for i in (1, 3, 2):
                bsend(s, 0, 1, i, ydev(i)).start()
                bsend(s, 1, 0, i, xdev(i)).start()
            bcore(s, tile).start()

    def b_forward(s):
        for j in (1, 3, 2):
            @pl.when(y < nb)
            def _():
                d = at(xp(j), y, core)
                await_b(s, d, 0)
                for i in (1, 3, 2):
                    bfwd(s, 0, j, i, d, ydev(i)).start()

            @pl.when(yp(j) < nb)
            def _():
                d = at(x, yp(j), core)
                await_b(s, d, 1)
                for i in (1, 3, 2):
                    bfwd(s, 1, j, i, d, xdev(i)).start()

    def rest_b(s, yy, d, zero, one):
        @pl.when(yy < nb)
        def _():
            if zero:
                await_b(s, d, 0)
            if one:
                await_b(s, d, 1)
            bcore(s, d).start()

    def b_rest(s):
        for j in (1, 2, 3):
            rest_b(s, y, at(xp(j), y, core), False, True)
            rest_b(s, yp(j), at(x, yp(j), core), True, False)
        for i in (1, 2, 3):
            for j in (1, 2, 3):
                rest_b(s, yp(i), at(xp(j), yp(i), core), True, True)

    def rest_a(d, zero, one):
        if zero:
            await_a(d, 0)
        if one:
            await_a(d, 1)
        acore(d).start()

    b_own(0)
    for j in (1, 2, 3):
        rest_a(at(xp(j), y, core), False, True)
        rest_a(at(x, yp(j), core), True, False)
    for i in (1, 2, 3):
        for j in (1, 2, 3):
            rest_a(at(xp(j), yp(i), core), True, True)
    b_forward(0)
    zup(2, (0,))
    zup(3, (0,))
    b_own(1)
    b_rest(0)
    for i in (1, 2, 3):
        lwaits(i)
    lists = [pltpu.make_async_copy(cols_v, cols_s, loc_sem.at[4]),
             pltpu.make_async_copy(tgts_v, tgts_s, loc_sem.at[5])]
    for cp in lists:
        cp.start()
    b_forward(1)
    b_rest(1)

    def from_core_a(n, _):
        d = n * 2 + 1 - core
        remote(whole(d), whole(d), a_csend.at[n], a_crecv.at[n], sib).wait_recv()
        return 0

    lax.fori_loop(0, NX * NY, from_core_a, 0)

    def from_core_b(n, _):
        d = n * 2 + 1 - core
        for s in (0, 1):
            remote(bwhole(s, d), bwhole(s, d), b_csend.at[s, n], b_crecv.at[s, n], sib).wait_recv()
        return 0

    lax.fori_loop(0, nb * NX, from_core_b, 0)
    for cp in lists:
        cp.wait()

    def left(p, o):
        total = None
        for k in range(0, 16, 2):
            am = jnp.concatenate([a_all[amp_s[k + s, lax.rem(mine, 128) + 2 * p + o]] for s in (0, 1)], axis=1)
            bm = jnp.concatenate([b_all[cols_s[p, o, k + s]] for s in (0, 1)], axis=1)
            term = lax.dot_general(am, bm, NT, preferred_element_type=jnp.float32)
            total = term if total is None else total + term
        return total.astype(jnp.bfloat16)

    def partial(p):
        both = [left(p, o) for o in (0, 1)]
        return [lax.dot_general(both[o], b_all[tgts_s[p, 0, o]], NN, preferred_element_type=jnp.float32) for o in (0, 1)]

    def rcopy(i, o):
        n = (i - 1) * 2 + o
        return remote(part_s.at[n], part_r.at[n], r_send.at[n], r_recv.at[n], ldev(i))

    def away(n, _):
        i = n + 1
        for o, r in enumerate(partial(lax.rem(pos + i, LINE))):
            part_s[2 * n + o] = r.astype(jnp.bfloat16)
            rcopy(i, o).start()
        return 0

    lax.fori_loop(0, LINE - 1, away, 0)
    for o, r in enumerate(partial(pos)):
        own[o] = r

    for i in (1, 2, 3):
        for o in (0, 1):
            rcopy(i, o).wait_recv()
    for o in range(2):
        out_ref[o] = (own[o] + part_r[o].astype(jnp.float32) + part_r[2 + o].astype(jnp.float32)
                      + part_r[4 + o].astype(jnp.float32)).astype(jnp.bfloat16)

    for i in (1, 2, 3):
        for o in (0, 1):
            rcopy(i, o).wait_send()
        for cp in lcopies(i):
            cp.wait_send()
        for h in (0, 1):
            asend(h, 0, i, xdev(i)).wait_send()
            asend(h, 1, i, ydev(i)).wait_send()
        for j in (1, 2, 3):
            afwd(0, j, i, at(xp(j), y, core), ydev(i)).wait_send()
            afwd(1, j, i, at(x, yp(j), core), xdev(i)).wait_send()

    def core_sent(n, _):
        acore(n * 2 + core).wait_send()
        return 0

    lax.fori_loop(0, NX * NY, core_sent, 0)

    def bcore_sent(n, _):
        for s in (0, 1):
            bcore(s, n * 2 + core).wait_send()
        return 0

    lax.fori_loop(0, nb * NX, bcore_sent, 0)

    @pl.when(y < nb)
    def _():
        for i in (1, 2, 3):
            zcopy(i).wait_send()
            for s in (0, 1):
                for h in (0, 1):
                    bsend(s, h, 0, i, xdev(i)).wait_send()
                    bsend(s, h, 1, i, ydev(i)).wait_send()
                for j in (1, 2, 3):
                    bfwd(s, 0, j, i, at(xp(j), y, core), ydev(i)).wait_send()

    for j in (1, 2, 3):
        @pl.when(yp(j) < nb)
        def _():
            for i in (1, 2, 3):
                for s in (0, 1):
                    bfwd(s, 1, j, i, at(x, yp(j), core), xdev(i)).wait_send()


def body(amplitudes, df_factors, out_tiles, pair_col, pair_amp):
    ts = amplitudes.shape[1]
    rows, cols = df_factors.shape
    ctiles = cols // ts
    pairs = pair_col.shape[1]
    dma = pltpu.SemaphoreType.DMA
    reg = pltpu.SemaphoreType.REGULAR
    chips = NX * NY
    anyw = pl.BlockSpec(memory_space=pl.ANY)
    return pl.pallas_call(
        kernel,
        out_shape=jax.ShapeDtypeStruct((2, ts, ts), jnp.bfloat16),
        in_specs=[anyw] * 5,
        out_specs=pl.BlockSpec(memory_space=pltpu.VMEM),
        scratch_shapes=[
            pltpu.VMEM((4 * 2 * chips, ts, ts), jnp.bfloat16),
            pltpu.VMEM((ctiles, QUAD * rows, ts), jnp.bfloat16),
            pltpu.VMEM((LINE, 2, pairs), jnp.int32),
            pltpu.VMEM((LINE, 1, 2), jnp.int32),
            pltpu.SMEM((pairs, 128), jnp.int32),
            pltpu.SMEM((LINE, 2, pairs), jnp.int32),
            pltpu.SMEM((LINE, 1, 2), jnp.int32),
            pltpu.VMEM((2, ts, ts), jnp.float32),
            pltpu.VMEM((6, ts, ts), jnp.bfloat16),
            pltpu.VMEM((6, ts, ts), jnp.bfloat16),
            dma((6 + ctiles,)), reg((4,)), reg((4,)), dma((4,)), dma((4,)), dma((2, 4)), dma((2, 4)),
            dma((2, 2, 4)), dma((2, 4, 4)), dma((chips,)), dma((2, chips)), dma((chips,)),
            dma((2, 2, 2, 4)), dma((2, 2, 4, 4)), dma((2, chips)), dma((2, 2, chips)), dma((2, chips)),
            dma((6,)), dma((6,)),
        ],
        compiler_params=pltpu.CompilerParams(
            collective_id=0, has_side_effects=True, vmem_limit_bytes=56 * 2**20),
        name="residual",
    )(pair_amp.T, pair_col, out_tiles[None], amplitudes, df_factors)


def solution(mesh):
    in_specs = (
        P("tile", None, None),
        P("aux", None),
        P(("tile", "aux")),
        P(("tile", "aux"), None),
        P(),
    )
    out_specs = P(("tile", "aux"), None, None)
    return jax.shard_map(body, mesh=mesh, in_specs=in_specs, out_specs=out_specs, check_vma=False)
```

time: 59.5 us -> 50.6 us (0.85)
  Pallas kernels: 55.1 us -> 48.5 us
  local copies, waits for them, and re-layouts: 4.12 us -> 1.47 us
    pallas_call x1, Pallas kernels: 55.1 us -> 48.5 us  [body(): pl.pallas_call(kernel, out_shape=jax.ShapeDtypeStruct((2, ts, ts), jnp.bf...]
    unnamed x12 -> x1, local copies, waits for them, and re-layouts: 3.97 us -> 1.47 us
where the time goes in v2:
time: 50.6 us; the launch traced here: 50 us
  Pallas kernels  48.5 us (96%)
  local copies, waits for them, and re-layouts  1.47 us (3%)
    pallas_call x1, Pallas kernels, body(): pl.pallas_call(kernel, out_shape=jax.ShapeDtypeStruct((2, ts, ts), jnp.bf...  48.5 us
    unnamed x1, local copies, waits for them, and re-layouts  1.47 us

profile of v2, /device:TPU:1, one launch (start us, length us, event | category | flops | bytes accessed | tf_op | source)
XLA Modules:
  0.0 50.0 jit_solution(3589413830021763213)
XLA Ops:
  0.0 48.5 %residual.1 = bf16[2,128,128]{2,1,0:T(8,128)(2,1)} custom-call(s32[16,1024]{1,0:T(8,128)} %bitcast.2, s32[2,16]{1,0:T(2,128)} %col_ref.1, s32[1,2]{1,0:T(1,128)} %bitcast.3, bf16[4,128,128]{2,1,0:T(8,128)(2,1)} %a_ref.1, bf16[96,3072]{1,0:T(8,128)(2,1)} %b_ref.1), custom_call_target="tpu_custom_call" | custom-call | tf_op jit(solution)/shard_map/residual/pallas_call | solution.py:386
  48.5 1.5 %copy.7 = bf16[2,128,128]{2,1,0:T(8,128)(2,1)} copy(bf16[2,128,128]{2,1,0:T(8,128)(2,1)} %residual.1) | data formatting | bytes 131072

commit v3 on v2

--- a/solution.py
+++ b/solution.py
@@ -33,8 +33,9 @@
     rows = b_ref.shape[0]
     ctiles = b_all.shape[0]
     nb = ctiles // (2 * NX)
-    first = (rows, 2 * rows)
-    count = (rows, 2 * rows)
+    first = (rows, 3 * rows)
+    count = (2 * rows, rows)
+    slot = (0, 1, 3, 2)
 
     def at(xx, yy, cc):
         return (yy * NX + xx) * 2 + cc
@@ -105,11 +106,11 @@
             signal(l_ack.at[LINE - i], ldev(i))
 
     def zcopy(i):
-        return remote(b_all.at[tile, pl.ds(0, rows)], b_all.at[tile, pl.ds(rows * (QUAD - i), rows)],
+        return remote(b_all.at[tile, pl.ds(0, rows)], b_all.at[tile, pl.ds(rows * slot[QUAD - i], rows)],
                       z_send.at[i], z_recv.at[QUAD - i], zdev(i))
 
     def zwait(r):
-        remote(b_all.at[tile, pl.ds(0, rows)], b_all.at[tile, pl.ds(rows * r, rows)],
+        remote(b_all.at[tile, pl.ds(0, rows)], b_all.at[tile, pl.ds(rows * slot[r], rows)],
                z_send.at[r], z_recv.at[r], zdev(r)).wait_recv()
 
     def zup(i, ranks):
@@ -176,8 +177,10 @@
         await_a(d, 1)
         for i in (1, 3, 2):
             afwd(1, j, i, d, xdev(i)).start()
-
-    zup(1, (0, 1, 2))
+        if j == 1:
+            zup(1, (2,))
+
+    zup(1, (0, 1))
     zup(2, (1,))
     for i in (1, 2, 3):
         @pl.when(pos + i < LINE)
@@ -207,7 +210,7 @@
     def b_own(s):
         @pl.when(y < nb)
         def _():
-            for r in ((1,), (2, 3))[s]:
+            for r in ((1, 3), (2,))[s]:
                 zwait(r)
             for i in (1, 3, 2):
                 bsend(s, 0, 0, i, xdev(i)).start()
@@ -257,17 +260,20 @@
             await_a(d, 1)
         acore(d).start()
 
-    b_own(0)
     for j in (1, 2, 3):
         rest_a(at(xp(j), y, core), False, True)
         rest_a(at(x, yp(j), core), True, False)
-    for i in (1, 2, 3):
-        for j in (1, 2, 3):
+    zup(3, (0,))
+    b_own(0)
+    for i in (1, 3, 2):
+        for j in (1, 3, 2):
             rest_a(at(xp(j), yp(i), core), True, True)
-    b_forward(0)
-    zup(2, (0,))
-    zup(3, (0,))
-    b_own(1)
+        if i == 1:
+            zup(2, (0,))
+        if i == 3:
+            b_forward(0)
+            b_own(1)
+    b_forward(1)
     b_rest(0)
     for i in (1, 2, 3):
         lwaits(i)
@@ -275,7 +281,6 @@
              pltpu.make_async_copy(tgts_v, tgts_s, loc_sem.at[5])]
     for cp in lists:
         cp.start()
-    b_forward(1)
     b_rest(1)
 
     def from_core_a(n, _):

time: 50.6 us -> 52.2 us (1.032)
  Pallas kernels: 48.5 us -> 50.5 us
    pallas_call x1, Pallas kernels: 48.5 us -> 50.5 us  [body(): pl.pallas_call(kernel, out_shape=jax.ShapeDtypeStruct((2, ts, ts), jnp.bf...]
where the time goes in v3:
time: 52.2 us; the launch traced here: 52 us
  Pallas kernels  50.5 us (97%)
  local copies, waits for them, and re-layouts  1.47 us (3%)
    pallas_call x1, Pallas kernels, body(): pl.pallas_call(kernel, out_shape=jax.ShapeDtypeStruct((2, ts, ts), jnp.bf...  50.5 us
    unnamed x1, local copies, waits for them, and re-layouts  1.47 us

profile of v3, /device:TPU:1, one launch (start us, length us, event | category | flops | bytes accessed | tf_op | source)
XLA Modules:
  0.0 52.0 jit_solution(11345571882549846719)
XLA Ops:
  0.0 50.5 %residual.1 = bf16[2,128,128]{2,1,0:T(8,128)(2,1)} custom-call(s32[16,1024]{1,0:T(8,128)} %bitcast.2, s32[2,16]{1,0:T(2,128)} %col_ref.1, s32[1,2]{1,0:T(1,128)} %bitcast.3, bf16[4,128,128]{2,1,0:T(8,128)(2,1)} %a_ref.1, bf16[96,3072]{1,0:T(8,128)(2,1)} %b_ref.1), custom_call_target="tpu_custom_call" | custom-call | tf_op jit(solution)/shard_map/residual/pallas_call | solution.py:391
  50.5 1.5 %copy.7 = bf16[2,128,128]{2,1,0:T(8,128)(2,1)} copy(bf16[2,128,128]{2,1,0:T(8,128)(2,1)} %residual.1) | data formatting | bytes 131072

commit v4 on v3

--- a/solution.py
+++ b/solution.py
@@ -18,9 +18,10 @@
 
 def kernel(amp_ref, col_ref, tgt_ref, a_ref, b_ref, out_ref,
            a_all, b_all, cols_v, tgts_v, amp_s, cols_s, tgts_s, own, part_s, part_r,
-           loc_sem, z_ack, l_ack, z_send, z_recv, l_send, l_recv,
+           loc_sem, p_ack, z_ack, l_ack, z_send, z_recv, l_send, l_recv,
            a_send, a_fsend, a_csend, a_recv, a_crecv,
            b_send, b_fsend, b_csend, b_recv, b_crecv,
+           f_send, f_csend, f_recv, f_crecv,
            r_send, r_recv):
     tile = lax.axis_index("tile")
     z = lax.axis_index("aux")
@@ -33,8 +34,6 @@
     rows = b_ref.shape[0]
     ctiles = b_all.shape[0]
     nb = ctiles // (2 * NX)
-    first = (rows, 3 * rows)
-    count = (2 * rows, rows)
     slot = (0, 1, 3, 2)
 
     def at(xx, yy, cc):
@@ -93,25 +92,27 @@
             signal(barrier, ldev(i))
     for cp in local:
         cp.start()
-    for cp in local:
-        cp.wait()
     pl.semaphore_wait(barrier, len(near) + rank + pos)
     for i in (1, 2, 3):
-        @pl.when(rank + i >= QUAD)
-        def _():
-            signal(z_ack.at[QUAD - i], zdev(i))
+        signal(p_ack, xdev(i))
+    for i in (1, 2, 3):
+        if i != 2:
+            @pl.when(rank + i >= QUAD)
+            def _():
+                signal(z_ack.at[QUAD - i], zdev(i))
 
         @pl.when(pos + i >= LINE)
         def _():
             signal(l_ack.at[LINE - i], ldev(i))
 
     def zcopy(i):
-        return remote(b_all.at[tile, pl.ds(0, rows)], b_all.at[tile, pl.ds(rows * slot[QUAD - i], rows)],
+        return remote(b_ref.at[:, pl.ds(pl.multiple_of(tile * 128, 128), 128)],
+                      b_all.at[tile, pl.ds(rows * slot[QUAD - i], rows)],
                       z_send.at[i], z_recv.at[QUAD - i], zdev(i))
 
     def zwait(r):
-        remote(b_all.at[tile, pl.ds(0, rows)], b_all.at[tile, pl.ds(rows * slot[r], rows)],
-               z_send.at[r], z_recv.at[r], zdev(r)).wait_recv()
+        rows_r = b_all.at[tile, pl.ds(rows * slot[r], rows)]
+        remote(rows_r, rows_r, z_send.at[r], z_recv.at[r], zdev(r)).wait_recv()
 
     def zup(i, ranks):
         for r in ranks:
@@ -122,6 +123,27 @@
                 @pl.when(y < nb)
                 def _():
                     zcopy(i).start()
+
+    def zpass(i, r):
+        rows_r = b_all.at[tile, pl.ds(rows * slot[r], rows)]
+        return remote(rows_r, b_all.at[tile, pl.ds(rows * slot[2], rows)], z_send.at[2], z_recv.at[2], zdev(i))
+
+    def on_rank(r, f):
+        @pl.when((rank == r) & (y < nb))
+        def _():
+            f()
+
+    def relay():
+        def one():
+            zwait(3)
+            zpass(1, 3).start()
+
+        def zero():
+            zwait(1)
+            zpass(3, 1).start()
+
+        on_rank(1, one)
+        on_rank(0, zero)
 
     for i in (2, 1, 3):
         @pl.when((rank + i >= QUAD) & (y < nb))
@@ -144,7 +166,7 @@
         return a_all.at[pl.ds(d * 4, 4)]
 
     def asend(h, k, i, dev):
-        return remote(apiece(tile, h), apiece(tile, h), a_send.at[h, k, i], a_recv.at[h, tile // 2], dev)
+        return remote(a_ref.at[pl.ds(2 * h, 2)], apiece(tile, h), a_send.at[h, k, i], a_recv.at[h, tile // 2], dev)
 
     def acore(d):
         return remote(whole(d), whole(d), a_csend.at[d // 2], a_crecv.at[d // 2], sib)
@@ -161,12 +183,14 @@
     for i in (1, 3, 2):
         asend(0, 1, i, ydev(i)).start()
         asend(1, 0, i, xdev(i)).start()
+    for cp in local[1:3]:
+        cp.wait()
     for i in (1, 2, 3):
         @pl.when(pos + i >= LINE)
         def _():
             for cp in lcopies(i):
                 cp.start()
-    acore(tile).start()
+    remote(a_ref, whole(tile), a_csend.at[tile // 2], a_crecv.at[tile // 2], sib).start()
 
     for j in (1, 3, 2):
         d = at(xp(j), y, core)
@@ -181,7 +205,8 @@
             zup(1, (2,))
 
     zup(1, (0, 1))
-    zup(2, (1,))
+    zup(3, (0,))
+    relay()
     for i in (1, 2, 3):
         @pl.when(pos + i < LINE)
         def _():
@@ -189,69 +214,106 @@
             for cp in lcopies(i):
                 cp.start()
 
-    def bpiece(s, d, h):
-        return b_all.at[d, pl.ds(first[s] + count[s] // 2 * h, count[s] // 2)]
-
-    def bwhole(s, d):
-        return b_all.at[d, pl.ds(first[s], count[s])]
-
-    def bsend(s, h, k, i, dev):
-        return remote(bpiece(s, tile, h), bpiece(s, tile, h), b_send.at[s, h, k, i], b_recv.at[s, h, tile // 2], dev)
-
-    def bcore(s, d):
-        return remote(bwhole(s, d), bwhole(s, d), b_csend.at[s, d // 2], b_crecv.at[s, d // 2], sib)
-
-    def await_b(s, d, h):
-        remote(bpiece(s, d, h), bpiece(s, d, h), b_send.at[s, 0, 0, 0], b_recv.at[s, h, d // 2], sib).wait_recv()
-
-    def bfwd(s, h, j, i, d, dev):
-        return remote(bpiece(s, d, h), bpiece(s, d, h), b_fsend.at[s, h, j, i], b_recv.at[s, h, d // 2], dev)
-
-    def b_own(s):
+    def bpiece(d, h):
+        return b_all.at[d, pl.ds(rows + rows * h, rows)]
+
+    def bnear(d):
+        return b_all.at[d, pl.ds(rows, 2 * rows)]
+
+    def bfar(d):
+        return b_all.at[d, pl.ds(3 * rows, rows)]
+
+    def bsend(h, k, i, dev):
+        return remote(bpiece(tile, h), bpiece(tile, h), b_send.at[h, k, i], b_recv.at[h, tile // 2], dev)
+
+    def bcore(d):
+        return remote(bnear(d), bnear(d), b_csend.at[d // 2], b_crecv.at[d // 2], sib)
+
+    def await_b(d, h):
+        remote(bpiece(d, h), bpiece(d, h), b_send.at[0, 0, 0], b_recv.at[h, d // 2], sib).wait_recv()
+
+    def bfwd(h, j, i, d, dev):
+        return remote(bpiece(d, h), bpiece(d, h), b_fsend.at[h, j, i], b_recv.at[h, d // 2], dev)
+
+    def b_own():
         @pl.when(y < nb)
         def _():
-            for r in ((1, 3), (2,))[s]:
-                zwait(r)
+            @pl.when(rank != 0)
+            def _():
+                zwait(1)
+
+            @pl.when(rank != 1)
+            def _():
+                zwait(3)
+
             for i in (1, 3, 2):
-                bsend(s, 0, 0, i, xdev(i)).start()
-                bsend(s, 1, 1, i, ydev(i)).start()
+                bsend(0, 0, i, xdev(i)).start()
+                bsend(1, 1, i, ydev(i)).start()
             for i in (1, 3, 2):
-                bsend(s, 0, 1, i, ydev(i)).start()
-                bsend(s, 1, 0, i, xdev(i)).start()
-            bcore(s, tile).start()
-
-    def b_forward(s):
+                bsend(0, 1, i, ydev(i)).start()
+                bsend(1, 0, i, xdev(i)).start()
+            bcore(tile).start()
+
+    def b_forward():
         for j in (1, 3, 2):
             @pl.when(y < nb)
             def _():
                 d = at(xp(j), y, core)
-                await_b(s, d, 0)
+                await_b(d, 0)
                 for i in (1, 3, 2):
-                    bfwd(s, 0, j, i, d, ydev(i)).start()
+                    bfwd(0, j, i, d, ydev(i)).start()
 
             @pl.when(yp(j) < nb)
             def _():
                 d = at(x, yp(j), core)
-                await_b(s, d, 1)
+                await_b(d, 1)
                 for i in (1, 3, 2):
-                    bfwd(s, 1, j, i, d, xdev(i)).start()
-
-    def rest_b(s, yy, d, zero, one):
+                    bfwd(1, j, i, d, xdev(i)).start()
+
+    def rest_b(yy, d, zero, one):
         @pl.when(yy < nb)
         def _():
             if zero:
-                await_b(s, d, 0)
+                await_b(d, 0)
             if one:
-                await_b(s, d, 1)
-            bcore(s, d).start()
-
-    def b_rest(s):
+                await_b(d, 1)
+            bcore(d).start()
+
+    def b_rest():
         for j in (1, 2, 3):
-            rest_b(s, y, at(xp(j), y, core), False, True)
-            rest_b(s, yp(j), at(x, yp(j), core), True, False)
+            rest_b(y, at(xp(j), y, core), False, True)
+            rest_b(yp(j), at(x, yp(j), core), True, False)
         for i in (1, 2, 3):
             for j in (1, 2, 3):
-                rest_b(s, yp(i), at(xp(j), yp(i), core), True, True)
+                rest_b(yp(i), at(xp(j), yp(i), core), True, True)
+
+    others = sorted(
+        ((i, j) for i in range(NX) for j in range(NY) if i + j),
+        key=lambda p: -min(p[0], NX - p[0]) - min(p[1], NY - p[1]))
+
+    def fsend(i, j):
+        return remote(bfar(tile), bfar(tile), f_send.at[NX * j + i], f_recv.at[tile // 2], (at(xp(i), yp(j), core), z))
+
+    def fcore(d):
+        return remote(bfar(d), bfar(d), f_csend.at[d // 2], f_crecv.at[d // 2], sib)
+
+    def f_own():
+        pl.semaphore_wait(p_ack, 3)
+
+        @pl.when(y < nb)
+        def _():
+            zwait(2)
+            for i, j in others:
+                fsend(i, j).start()
+            fcore(tile).start()
+
+    def f_rest():
+        for i, j in reversed(others):
+            @pl.when(yp(j) < nb)
+            def _():
+                d = at(xp(i), yp(j), core)
+                remote(bfar(d), bfar(d), f_send.at[0], f_recv.at[d // 2], sib).wait_recv()
+                fcore(d).start()
 
     def rest_a(d, zero, one):
         if zero:
@@ -260,28 +322,32 @@
             await_a(d, 1)
         acore(d).start()
 
+    b_own()
     for j in (1, 2, 3):
         rest_a(at(xp(j), y, core), False, True)
         rest_a(at(x, yp(j), core), True, False)
-    zup(3, (0,))
-    b_own(0)
+
+    @pl.when(rank == 0)
+    def _():
+        b_forward()
+
+    f_own()
+
+    @pl.when(rank != 0)
+    def _():
+        b_forward()
+
     for i in (1, 3, 2):
         for j in (1, 3, 2):
             rest_a(at(xp(j), yp(i), core), True, True)
-        if i == 1:
-            zup(2, (0,))
-        if i == 3:
-            b_forward(0)
-            b_own(1)
-    b_forward(1)
-    b_rest(0)
+    b_rest()
     for i in (1, 2, 3):
         lwaits(i)
     lists = [pltpu.make_async_copy(cols_v, cols_s, loc_sem.at[4]),
              pltpu.make_async_copy(tgts_v, tgts_s, loc_sem.at[5])]
     for cp in lists:
         cp.start()
-    b_rest(1)
+    f_rest()
 
     def from_core_a(n, _):
         d = n * 2 + 1 - core
@@ -292,12 +358,12 @@
 
     def from_core_b(n, _):
         d = n * 2 + 1 - core
-        for s in (0, 1):
-            remote(bwhole(s, d), bwhole(s, d), b_csend.at[s, n], b_crecv.at[s, n], sib).wait_recv()
+        remote(bnear(d), bnear(d), b_csend.at[n], b_crecv.at[n], sib).wait_recv()
+        remote(bfar(d), bfar(d), f_csend.at[n], f_crecv.at[n], sib).wait_recv()
         return 0
 
     lax.fori_loop(0, nb * NX, from_core_b, 0)
-    for cp in lists:
+    for cp in lists + local[:1] + local[3:]:
         cp.wait()
 
     def left(p, o):
@@ -317,14 +383,12 @@
         n = (i - 1) * 2 + o
         return remote(part_s.at[n], part_r.at[n], r_send.at[n], r_recv.at[n], ldev(i))
 
-    def away(n, _):
-        i = n + 1
-        for o, r in enumerate(partial(lax.rem(pos + i, LINE))):
-            part_s[2 * n + o] = r.astype(jnp.bfloat16)
+    upper = pos // 2
+    for dest in (3 * (1 - upper), 2 - upper, pos + 1 - 2 * lax.rem(pos, 2)):
+        i = lax.rem(dest - pos + LINE, LINE)
+        for o, r in enumerate(partial(dest)):
+            part_s[2 * i - 2 + o] = r.astype(jnp.bfloat16)
             rcopy(i, o).start()
-        return 0
-
-    lax.fori_loop(0, LINE - 1, away, 0)
     for o, r in enumerate(partial(pos)):
         own[o] = r
 
@@ -354,29 +418,29 @@
     lax.fori_loop(0, NX * NY, core_sent, 0)
 
     def bcore_sent(n, _):
-        for s in (0, 1):
-            bcore(s, n * 2 + core).wait_send()
+        bcore(n * 2 + core).wait_send()
+        fcore(n * 2 + core).wait_send()
         return 0
 
     lax.fori_loop(0, nb * NX, bcore_sent, 0)
 
     @pl.when(y < nb)
     def _():
+        for i, j in others:
+            fsend(i, j).wait_send()
         for i in (1, 2, 3):
             zcopy(i).wait_send()
-            for s in (0, 1):
-                for h in (0, 1):
-                    bsend(s, h, 0, i, xdev(i)).wait_send()
-                    bsend(s, h, 1, i, ydev(i)).wait_send()
-                for j in (1, 2, 3):
-                    bfwd(s, 0, j, i, at(xp(j), y, core), ydev(i)).wait_send()
+            for h in (0, 1):
+                bsend(h, 0, i, xdev(i)).wait_send()
+                bsend(h, 1, i, ydev(i)).wait_send()
+            for j in (1, 2, 3):
+                bfwd(0, j, i, at(xp(j), y, core), ydev(i)).wait_send()
 
     for j in (1, 2, 3):
         @pl.when(yp(j) < nb)
         def _():
             for i in (1, 2, 3):
-                for s in (0, 1):
-                    bfwd(s, 1, j, i, at(x, yp(j), core), xdev(i)).wait_send()
+                bfwd(1, j, i, at(x, yp(j), core), xdev(i)).wait_send()
 
 
 def body(amplitudes, df_factors, out_tiles, pair_col, pair_amp):
@@ -404,9 +468,10 @@
             pltpu.VMEM((2, ts, ts), jnp.float32),
             pltpu.VMEM((6, ts, ts), jnp.bfloat16),
             pltpu.VMEM((6, ts, ts), jnp.bfloat16),
-            dma((6 + ctiles,)), reg((4,)), reg((4,)), dma((4,)), dma((4,)), dma((2, 4)), dma((2, 4)),
+            dma((6 + ctiles,)), reg, reg((4,)), reg((4,)), dma((4,)), dma((4,)), dma((2, 4)), dma((2, 4)),
             dma((2, 2, 4)), dma((2, 4, 4)), dma((chips,)), dma((2, chips)), dma((chips,)),
-            dma((2, 2, 2, 4)), dma((2, 2, 4, 4)), dma((2, chips)), dma((2, 2, chips)), dma((2, chips)),
+            dma((2, 2, 4)), dma((2, 4, 4)), dma((chips,)), dma((2, chips)), dma((chips,)),
+            dma((chips,)), dma((chips,)), dma((chips,)), dma((chips,)),
             dma((6,)), dma((6,)),
         ],
         compiler_params=pltpu.CompilerParams(

time: 52.2 us -> 48.4 us (0.927)
  Pallas kernels: 50.5 us -> 46.6 us
    pallas_call x1, Pallas kernels: 50.5 us -> 46.6 us  [body(): pl.pallas_call(kernel, out_shape=jax.ShapeDtypeStruct((2, ts, ts), jnp.bf...]
where the time goes in v4:
time: 48.4 us; the launch traced here: 48 us
  Pallas kernels  46.6 us (96%)
  local copies, waits for them, and re-layouts  1.47 us (3%)
    pallas_call x1, Pallas kernels, body(): pl.pallas_call(kernel, out_shape=jax.ShapeDtypeStruct((2, ts, ts), jnp.bf...  46.6 us
    unnamed x1, local copies, waits for them, and re-layouts  1.47 us

profile of v4, /device:TPU:1, one launch (start us, length us, event | category | flops | bytes accessed | tf_op | source)
XLA Modules:
  0.0 48.0 jit_solution(4150196779558724306)
XLA Ops:
  0.0 46.6 %residual.1 = bf16[2,128,128]{2,1,0:T(8,128)(2,1)} custom-call(s32[16,1024]{1,0:T(8,128)} %bitcast.2, s32[2,16]{1,0:T(2,128)} %col_ref.1, s32[1,2]{1,0:T(1,128)} %bitcast.3, bf16[4,128,128]{2,1,0:T(8,128)(2,1)} %a_ref.1, bf16[96,3072]{1,0:T(8,128)(2,1)} %b_ref.1), custom_call_target="tpu_custom_call" | custom-call | tf_op jit(solution)/shard_map/residual/pallas_call | solution.py:455
  46.6 1.5 %copy.7 = bf16[2,128,128]{2,1,0:T(8,128)(2,1)} copy(bf16[2,128,128]{2,1,0:T(8,128)(2,1)} %residual.1) | data formatting | bytes 131072

commit v5 on v4

--- a/solution.py
+++ b/solution.py
@@ -384,13 +384,30 @@
         return remote(part_s.at[n], part_r.at[n], r_send.at[n], r_recv.at[n], ldev(i))
 
     upper = pos // 2
-    for dest in (3 * (1 - upper), 2 - upper, pos + 1 - 2 * lax.rem(pos, 2)):
+
+    def one_dest(n, _):
+        last = n // 3
+        third = n // 2 - last
+        second = lax.rem(n, 2) - last
+        dest = ((1 - second - third - last) * 3 * (1 - upper) + second * (2 - upper)
+                + third * (pos + 1 - 2 * lax.rem(pos, 2)) + last * pos)
         i = lax.rem(dest - pos + LINE, LINE)
-        for o, r in enumerate(partial(dest)):
-            part_s[2 * i - 2 + o] = r.astype(jnp.bfloat16)
-            rcopy(i, o).start()
-    for o, r in enumerate(partial(pos)):
-        own[o] = r
+        both = partial(dest)
+
+        @pl.when(n < LINE - 1)
+        def _():
+            for o, r in enumerate(both):
+                part_s[2 * i - 2 + o] = r.astype(jnp.bfloat16)
+                rcopy(i, o).start()
+
+        @pl.when(n == LINE - 1)
+        def _():
+            for o, r in enumerate(both):
+                own[o] = r
+
+        return 0
+
+    lax.fori_loop(0, LINE, one_dest, 0)
 
     for i in (1, 2, 3):
         for o in (0, 1):
@@ -475,7 +492,7 @@
             dma((6,)), dma((6,)),
         ],
         compiler_params=pltpu.CompilerParams(
-            collective_id=0, has_side_effects=True, vmem_limit_bytes=56 * 2**20),
+            collective_id=0, has_side_effects=True, vmem_limit_bytes=861 * 2**16),
         name="residual",
     )(pair_amp.T, pair_col, out_tiles[None], amplitudes, df_factors)
 

time: 48.4 us -> 47.5 us (0.981)
  Pallas kernels: 46.6 us -> 46 us
    pallas_call x1, Pallas kernels: 46.6 us -> 46 us  [body(): pl.pallas_call(kernel, out_shape=jax.ShapeDtypeStruct((2, ts, ts), jnp.bf...]
    unnamed x1 -> x5, local copies, waits for them, and re-layouts: 1.47 us -> 1.31 us
where the time goes in v5:
time: 47.5 us; the launch traced here: 47.3 us
  Pallas kernels  46 us (97%)
  local copies, waits for them, and re-layouts  1.31 us (3%)
    pallas_call x1, Pallas kernels, body(): pl.pallas_call(kernel, out_shape=jax.ShapeDtypeStruct((2, ts, ts), jnp.bf...  46 us
    unnamed x5, local copies, waits for them, and re-layouts  1.31 us

profile of v5, /device:TPU:1, one launch (start us, length us, event | category | flops | bytes accessed | tf_op | source)
XLA Modules:
  0.0 47.3 jit_solution(4427349926869509280)
XLA Ops:
  0.0 0.0 copy-start
  0.0 0.0 copy-start.1
  0.0 0.7 %copy-done = s32[2,16]{1,0:T(2,128)S(1)} copy-done((s32[2,16]{1,0:T(2,128)S(1)}, s32[2,16]{1,0:T(2,128)}, u32[]{:S(2)}) %copy-start) | copy-done | bytes 152
  0.7 0.0 copy-done.1
  0.7 46.0 %residual.1 = bf16[2,128,128]{2,1,0:T(8,128)(2,1)S(1)} custom-call(s32[16,1024]{1,0:T(8,128)} %bitcast.3, s32[2,16]{1,0:T(2,128)S(1)} %copy-done, s32[1,2]{1,0:T(1,128)S(1)} %bitcast.2, bf16[4,128,128]{2,1,0:T(8,128)(2,1)} %a_ref.1, bf16[96,3072]{1,0:T(8,128)(2,1)} %b_ref.1), custom_call_target="tpu_custom_call" | custom-call | tf_op jit(solution)/shard_map/residual/pallas_call | solution.py:472
  46.7 0.6 %copy.7 = bf16[2,128,128]{2,1,0:T(8,128)(2,1)} copy(bf16[2,128,128]{2,1,0:T(8,128)(2,1)S(1)} %residual.1) | data formatting | bytes 131072
Async XLA Ops:
  0.0 0.7 %copy-start = (s32[2,16]{1,0:T(2,128)S(1)}, s32[2,16]{1,0:T(2,128)}, u32[]{:S(2)}) copy-start(s32[2,16]{1,0:T(2,128)} %col_ref.1) | copy-start | bytes 388
  0.0 0.7 %copy-start.1 = (s32[2]{0:T(128)S(1)}, s32[2]{0:T(128)}, u32[]{:S(2)}) copy-start(s32[2]{0:T(128)} %param.7) | copy-start | bytes 28

commit v6 on v5

--- a/solution.py
+++ b/solution.py
@@ -410,15 +410,6 @@
     lax.fori_loop(0, LINE, one_dest, 0)
 
     for i in (1, 2, 3):
-        for o in (0, 1):
-            rcopy(i, o).wait_recv()
-    for o in range(2):
-        out_ref[o] = (own[o] + part_r[o].astype(jnp.float32) + part_r[2 + o].astype(jnp.float32)
-                      + part_r[4 + o].astype(jnp.float32)).astype(jnp.bfloat16)
-
-    for i in (1, 2, 3):
-        for o in (0, 1):
-            rcopy(i, o).wait_send()
         for cp in lcopies(i):
             cp.wait_send()
         for h in (0, 1):
@@ -458,6 +449,16 @@
         def _():
             for i in (1, 2, 3):
                 bfwd(1, j, i, at(x, yp(j), core), xdev(i)).wait_send()
+
+    for i in (1, 2, 3):
+        for o in (0, 1):
+            rcopy(i, o).wait_recv()
+    for o in range(2):
+        out_ref[o] = (own[o] + part_r[o].astype(jnp.float32) + part_r[2 + o].astype(jnp.float32)
+                      + part_r[4 + o].astype(jnp.float32)).astype(jnp.bfloat16)
+    for i in (1, 2, 3):
+        for o in (0, 1):
+            rcopy(i, o).wait_send()
 
 
 def body(amplitudes, df_factors, out_tiles, pair_col, pair_amp):

time: 47.5 us -> 46.9 us (0.987)
  Pallas kernels: 46 us -> 45.4 us
    pallas_call x1, Pallas kernels: 46 us -> 45.4 us  [body(): pl.pallas_call(kernel, out_shape=jax.ShapeDtypeStruct((2, ts, ts), jnp.bf...]
where the time goes in v6:
time: 46.9 us; the launch traced here: 46.8 us
  Pallas kernels  45.4 us (97%)
  local copies, waits for them, and re-layouts  1.31 us (3%)
    pallas_call x1, Pallas kernels, body(): pl.pallas_call(kernel, out_shape=jax.ShapeDtypeStruct((2, ts, ts), jnp.bf...  45.4 us
    unnamed x5, local copies, waits for them, and re-layouts  1.31 us

profile of v6, /device:TPU:1, one launch (start us, length us, event | category | flops | bytes accessed | tf_op | source)
XLA Modules:
  0.0 46.8 jit_solution(5457372843282553418)
XLA Ops:
  0.0 0.0 copy-start
  0.0 0.0 copy-start.1
  0.0 0.7 %copy-done = s32[2,16]{1,0:T(2,128)S(1)} copy-done((s32[2,16]{1,0:T(2,128)S(1)}, s32[2,16]{1,0:T(2,128)}, u32[]{:S(2)}) %copy-start) | copy-done | bytes 152
  0.7 0.0 copy-done.1
  0.7 45.4 %residual.1 = bf16[2,128,128]{2,1,0:T(8,128)(2,1)S(1)} custom-call(s32[16,1024]{1,0:T(8,128)} %bitcast.3, s32[2,16]{1,0:T(2,128)S(1)} %copy-done, s32[1,2]{1,0:T(1,128)S(1)} %bitcast.2, bf16[4,128,128]{2,1,0:T(8,128)(2,1)} %a_ref.1, bf16[96,3072]{1,0:T(8,128)(2,1)} %b_ref.1), custom_call_target="tpu_custom_call" | custom-call | tf_op jit(solution)/shard_map/residual/pallas_call | solution.py:473
  46.1 0.6 %copy.7 = bf16[2,128,128]{2,1,0:T(8,128)(2,1)} copy(bf16[2,128,128]{2,1,0:T(8,128)(2,1)S(1)} %residual.1) | data formatting | bytes 131072
Async XLA Ops:
  0.0 0.7 %copy-start = (s32[2,16]{1,0:T(2,128)S(1)}, s32[2,16]{1,0:T(2,128)}, u32[]{:S(2)}) copy-start(s32[2,16]{1,0:T(2,128)} %col_ref.1) | copy-start | bytes 388
  0.0 0.7 %copy-start.1 = (s32[2]{0:T(128)S(1)}, s32[2]{0:T(128)}, u32[]{:S(2)}) copy-start(s32[2]{0:T(128)} %param.7) | copy-start | bytes 28
